TPU v7x, 32 devices: a whole 2x2x4 slice. The times are simulated.
32 devices in a mesh: grp: 2 (over x), row: 8 (over z, y), col: 2 (over core).
Axes of the slice: x: 2, y: 2, z: 4, core: 2. Of those that a mesh axis runs over, the one named last changes fastest.
Arguments:
- pair: float32 [1024, 512, 128], P(('grp', 'row'), 'col'), parts along dimension 0, may hold values from -400 to 400
- token_count: int32 [2], P('grp'), parts along dimension 0, may hold values from 256 to 512
- chain_ids: int32 [1024], P('grp'), parts along dimension 0, may hold values from 0 to 5, never falling along the last dimension, each value on 1 to 170 neighbouring positions
- chain_term: float32 [128], replicated, may hold values from -4 to 4
- in_gain: float32 [2, 128], replicated, may hold values from 0.25 to 1.75
- in_bias: float32 [2, 128], replicated, may hold values from -3 to 3
- proj: bfloat16 [2, 128, 512], replicated, may hold values from -0.5 to 0.5
- gate_w: bfloat16 [2, 128, 128], replicated, may hold values from -0.5 to 0.5
- hid_gain: float32 [2, 128], replicated, may hold values from 0.25 to 1.75
- hid_bias: float32 [2, 128], replicated, may hold values from -3 to 3
- out_w: bfloat16 [2, 128, 128], replicated, may hold values from -0.5 to 0.5
Outputs:
- pair_out: float32 [1024, 512, 128], P(('grp', 'row'), 'col'), parts along dimension 0
There are 2 independent parts, one for each index of `grp`. A program takes and returns all parts, laid end to end along the dimension named above; an argument that names none is the same for every part. Nothing has to cross between parts.
Inputs may be any that keep to these rules, and one draw needn't show every extreme that they name: `token_count`: tokens at positions below the count are real, the rest are padding. `chain_ids`: chain numbers never fall along the tokens.
All inputs are finite; a program needn't handle non-finite values.
Results may differ from a plain program's by a relative error of at most 0.0011.
Values may be sent and summed in bfloat16 or wider, within the bound.
A program may use at most 192 MiB of HBM per device.

v0:
```python
import jax
import jax.numpy as jnp
from jax import lax
from jax.sharding import PartitionSpec as P

EPSILON = 1e-05


def norm_last(values, gain, bias):
    center = values - jnp.mean(values, axis=-1, keepdims=True)
    variance = jnp.mean(center * center, axis=-1, keepdims=True)
    return center * lax.rsqrt(variance + EPSILON) * gain + bias


def norm_first(values, gain, bias):
    center = values - jnp.mean(values, axis=0, keepdims=True)
    variance = jnp.mean(center * center, axis=0, keepdims=True)
    return center * lax.rsqrt(variance + EPSILON) * gain[:, None, None] + bias[:, None, None]


def channel_product(left_full, right_full, outgoing):
    if outgoing:
        result = jnp.einsum(
            "cik,cjk->cij", left_full, right_full, preferred_element_type=jnp.float32
        )
    else:
        result = jnp.einsum(
            "cki,ckj->cij", left_full, right_full, preferred_element_type=jnp.float32
        )
    return result.astype(jnp.bfloat16)


def triangle(left_side, right_side, outgoing):
    hidden, rows_here, cols_here = left_side.shape
    row_count = lax.axis_size("row")
    col_count = lax.axis_size("col")
    left_recv, right_recv = (
        lax.all_to_all(left_side, ("row", "col"), split_axis=0, concat_axis=1, tiled=True),
        lax.all_to_all(right_side, ("row", "col"), split_axis=0, concat_axis=1, tiled=True),
    )
    per_device = left_recv.shape[0]

    def spread(values):
        values = values.reshape(per_device, row_count, col_count, rows_here, cols_here)
        return values.transpose(0, 1, 3, 2, 4).reshape(
            per_device, row_count * rows_here, col_count * cols_here
        )

    mixed = channel_product(spread(left_recv), spread(right_recv), outgoing)
    packed = mixed.reshape(per_device, row_count, rows_here, col_count, cols_here)
    packed = packed.transpose(0, 1, 3, 2, 4).reshape(
        per_device, row_count * col_count * rows_here, cols_here
    )
    return lax.all_to_all(packed, ("row", "col"), split_axis=1, concat_axis=0, tiled=True)


def body(
    pair,
    token_count,
    chain_ids,
    chain_term,
    in_gain,
    in_bias,
    proj,
    gate_w,
    hid_gain,
    hid_bias,
    out_w,
):
    rows_here, cols_here, pair_width = pair.shape
    hidden = proj.shape[2] // 4
    tokens_all = chain_ids.shape[0]
    row_first = lax.axis_index("row") * rows_here
    col_first = lax.axis_index("col") * cols_here
    positions = jnp.arange(tokens_all, dtype=jnp.int32)
    token_valid = (positions < token_count[0]).astype(jnp.float32)
    row_valid = lax.dynamic_slice_in_dim(token_valid, row_first, rows_here, 0)
    col_valid = lax.dynamic_slice_in_dim(token_valid, col_first, cols_here, 0)
    row_chain = lax.dynamic_slice_in_dim(chain_ids, row_first, rows_here, 0)
    col_chain = lax.dynamic_slice_in_dim(chain_ids, col_first, cols_here, 0)
    same_chain = (row_chain[:, None] == col_chain[None, :]).astype(jnp.float32)
    pair_mask = row_valid[:, None] * col_valid[None, :]
    state = pair + same_chain[:, :, None] * chain_term
    for layer_index in range(2):
        normed = norm_last(state, in_gain[layer_index], in_bias[layer_index]).astype(jnp.bfloat16)
        hidden_all = jnp.einsum(
            "ijc,cf->fij", normed, proj[layer_index], preferred_element_type=jnp.float32
        )
        left_side = (
            pair_mask * jax.nn.sigmoid(hidden_all[:hidden]) * hidden_all[hidden : 2 * hidden]
        ).astype(jnp.bfloat16)
        right_side = (
            pair_mask
            * jax.nn.sigmoid(hidden_all[2 * hidden : 3 * hidden])
            * hidden_all[3 * hidden :]
        ).astype(jnp.bfloat16)
        gate_value = jax.nn.sigmoid(
            jnp.einsum(
                "ijc,cd->ijd", normed, gate_w[layer_index], preferred_element_type=jnp.float32
            )
        )
        mixed = triangle(left_side, right_side, layer_index == 0)
        normed_mix = norm_first(
            mixed.astype(jnp.float32), hid_gain[layer_index], hid_bias[layer_index]
        ).astype(jnp.bfloat16)
        update = jnp.einsum(
            "hij,hc->ijc", normed_mix, out_w[layer_index], preferred_element_type=jnp.float32
        )
        state = state + gate_value * update
    return state


def solution(mesh):
    return jax.shard_map(
        body,
        mesh=mesh,
        in_specs=(
            P(("grp", "row"), "col", None),
            P("grp"),
            P("grp"),
            P(),
            P(),
            P(),
            P(),
            P(),
            P(),
            P(),
            P(),
        ),
        out_specs=P(("grp", "row"), "col", None),
        check_vma=False,
    )
```

profile of v0, /device:TPU:13, one launch (start us, length us, event | category | flops | bytes accessed | tf_op | source)
XLA Modules:
  0.0 816.6 jit_solution(12445312548826828160)
XLA Ops:
  2.3 9.0 %copy.82 = f32[64,256,128]{1,2,0:T(8,128)} copy(f32[64,256,128]{2,1,0:T(8,128)} %param.11) | data formatting | bytes 16777216 | tf_op args[0]
  11.4 5.3 fusion.36
  17.1 2.4 multiply_reduce_fusion.1
  19.7 17.4 %convolution_bitcast_fusion.1 = f32[512,64,256]{0,2,1:T(8,128)} fusion(bf16[2,128,512]{2,1,0:T(8,128)(2,1)S(1)} %copy-done.2, f32[64,256,128]{1,2,0:T(8,128)} %copy.82, f32[128]{0:T(128)S(1)} %get-tuple-element.16, f32[128]{0:T(128)S(1)} %get-tuple-element.21, f32[64,256]{1,0:T(8,128)S(1)} %add_rsqrt_fusion.3, f32[64,256]{1,0:T(8,128)S(1)} %broadcast_multiply_fusion.4, ...), kind=kOutput, calls=%fused_computation.1 | convolution fusion | flops 2162163712 | bytes 42272256 | tf_op jit(solution)/shard_map/ijc,cf->fij/dot_general | solution.py:86
  37.1 15.4 %fusion.10 = (bf16[128,64,256]{0,2,1:T(8,128)(2,1)}, bf16[128,64,256]{0,2,1:T(8,128)(2,1)}) fusion(f32[512,64,256]{0,2,1:T(8,128)} %convolution_bitcast_fusion.1, f32[64,256]{1,0:T(8,128)S(1)} %broadcast_multiply_fusion), kind=kLoop, calls=%fused_computation.17 | loop fusion | flops 25165824 | bytes 42008576 | tf_op jit(solution)/shard_map/convert_element_type | solution.py:96
  52.4 6.9 copy.86
  59.3 6.6 all-to-all-start
  65.8 6.8 copy.88
  72.7 85.6 %all-to-all-done = bf16[128,64,256]{2,1,0:T(8,128)(2,1)} async-done(((bf16[128,64,256]{2,1,0:T(8,128)(2,1)}), bf16[128,64,256]{2,1,0:T(8,128)(2,1)}, u32[]{:S(2)}, u32[]{:S(2)}) %all-to-all-start) | async-done | bytes 4194336 | tf_op jit(solution)/shard_map/all_to_all | solution.py:38
  158.3 5.3 all-to-all-start.1
  163.6 8.6 %copy.139 = bf16[8,8,2,64,256]{4,2,3,1,0:T(2,128)(2,1)} copy(bf16[8,8,2,64,256]{4,3,0,2,1:T(8,128)(2,1)} %bitcast.10) | data formatting | bytes 8388608 | tf_op jit(solution)/shard_map/reshape | solution.py:44
  172.2 7.6 reshape.167
  179.8 76.2 %all-to-all-done.1 = bf16[128,64,256]{2,1,0:T(8,128)(2,1)} async-done(((bf16[128,64,256]{2,1,0:T(8,128)(2,1)}), bf16[128,64,256]{2,1,0:T(8,128)(2,1)}, u32[]{:S(2)}, u32[]{:S(2)}) %all-to-all-start.1) | async-done | bytes 4194336 | tf_op jit(solution)/shard_map/all_to_all | solution.py:39
  255.9 8.6 %copy.138 = bf16[8,8,2,64,256]{4,2,3,1,0:T(2,128)(2,1)} copy(bf16[8,8,2,64,256]{4,3,0,2,1:T(8,128)(2,1)} %bitcast.14) | data formatting | bytes 8388608 | tf_op jit(solution)/shard_map/reshape | solution.py:44
  264.5 7.6 reshape.169
  272.1 7.8 convolution_convert_fusion.1
  279.9 7.4 reshape.170
  287.3 6.7 copy.122
  294.0 4.9 all-to-all-start.2
  299.3 92.1 %all-to-all-done.2 = bf16[8,1024,256]{2,0,1:T(8,128)(2,1)} async-done(((bf16[8,1024,256]{2,0,1:T(8,128)(2,1)}), bf16[8,1024,256]{2,0,1:T(8,128)(2,1)}, u32[]{:S(2)}, u32[]{:S(2)}) %all-to-all-start.2) | async-done | bytes 4194336 | tf_op jit(solution)/shard_map/all_to_all | solution.py:54
  391.4 3.1 copy.92
  396.3 3.6 fusion.35
  400.5 6.5 fusion.39
  407.0 7.5 fusion.54
  414.5 3.4 copy-done.1
  417.8 1.8 multiply_reduce_fusion
  419.6 17.2 %convolution_bitcast_fusion = f32[512,64,256]{0,2,1:T(8,128)} fusion(bf16[2,128,512]{2,1,0:T(8,128)(2,1)S(1)} %copy-done.2, f32[64,256,128]{1,2,0:T(8,128)} %copy-done.1, f32[128]{0:T(128)S(1)} %get-tuple-element.15, f32[128]{0:T(128)S(1)} %get-tuple-element.22, f32[64,256]{1,0:T(8,128)S(1)} %add_rsqrt_fusion.1, f32[64,256]{1,0:T(8,128)S(1)} %broadcast_multiply_fusion.2), kind=kOutput, calls=%fused_computation | convolution fusion | flops 2157969408 | bytes 42206208 | tf_op jit(solution)/shard_map/ijc,cf->fij/dot_general | solution.py:86
  436.9 15.4 %fusion = (bf16[128,64,256]{0,2,1:T(8,128)(2,1)}, bf16[128,64,256]{0,2,1:T(8,128)(2,1)}) fusion(f32[512,64,256]{0,2,1:T(8,128)} %convolution_bitcast_fusion, f32[64,256]{1,0:T(8,128)S(1)} %broadcast_multiply_fusion), kind=kLoop, calls=%fused_computation.3 | loop fusion | flops 25165824 | bytes 42008576 | tf_op jit(solution)/shard_map/convert_element_type | solution.py:96
  452.2 6.9 copy.101
  459.1 4.9 all-to-all-start.3
  464.0 6.8 copy.103
  470.8 85.6 %all-to-all-done.3 = bf16[128,64,256]{2,1,0:T(8,128)(2,1)} async-done(((bf16[128,64,256]{2,1,0:T(8,128)(2,1)}), bf16[128,64,256]{2,1,0:T(8,128)(2,1)}, u32[]{:S(2)}, u32[]{:S(2)}) %all-to-all-start.3) | async-done | bytes 4194336 | tf_op jit(solution)/shard_map/all_to_all | solution.py:38
  556.5 4.9 all-to-all-start.4
  561.4 8.6 %copy.137 = bf16[8,8,2,64,256]{4,2,3,1,0:T(2,128)(2,1)} copy(bf16[8,8,2,64,256]{4,3,0,2,1:T(8,128)(2,1)} %bitcast.34) | data formatting | bytes 8388608 | tf_op jit(solution)/shard_map/reshape | solution.py:44
  569.9 7.6 reshape.173
  577.5 76.3 %all-to-all-done.4 = bf16[128,64,256]{2,1,0:T(8,128)(2,1)} async-done(((bf16[128,64,256]{2,1,0:T(8,128)(2,1)}), bf16[128,64,256]{2,1,0:T(8,128)(2,1)}, u32[]{:S(2)}, u32[]{:S(2)}) %all-to-all-start.4) | async-done | bytes 4194336 | tf_op jit(solution)/shard_map/all_to_all | solution.py:39
  653.8 8.6 %copy.136 = bf16[8,8,2,64,256]{4,2,3,1,0:T(2,128)(2,1)} copy(bf16[8,8,2,64,256]{4,3,0,2,1:T(8,128)(2,1)} %bitcast.38) | data formatting | bytes 8388608 | tf_op jit(solution)/shard_map/reshape | solution.py:44
  662.4 7.8 reshape.175
  670.2 7.8 convolution_convert_fusion
  678.0 6.9 reshape.176
  685.0 6.7 copy.123
  691.7 4.9 all-to-all-start.5
  696.9 92.2 %all-to-all-done.5 = bf16[8,1024,256]{2,0,1:T(8,128)(2,1)} async-done(((bf16[8,1024,256]{2,0,1:T(8,128)(2,1)}), bf16[8,1024,256]{2,0,1:T(8,128)(2,1)}, u32[]{:S(2)}, u32[]{:S(2)}) %all-to-all-start.5) | async-done | bytes 4194336 | tf_op jit(solution)/shard_map/all_to_all | solution.py:54
  789.1 3.1 copy.108
  793.9 3.6 fusion.27
  798.1 3.2 fusion.37
  801.3 5.9 multiply_add_fusion
  807.3 9.0 %copy.114 = f32[64,256,128]{2,1,0:T(8,128)} copy(f32[64,256,128]{1,2,0:T(8,128)} %multiply_add_fusion) | data formatting | bytes 16777216 | tf_op jit(solution)/shard_map/add | solution.py:109
  (60 shorter events, 7.7 us)
Async XLA Ops:
  2.3 9.1 %copy-start.4 = (f32[128]{0:T(128)S(1)}, f32[128]{0:T(128)}, u32[]{:S(2)}) copy-start(f32[128]{0:T(128)} %param.14) | copy-start | bytes 1540
  11.3 5.8 copy-start
  11.4 8.1 copy-start.5
  11.4 8.1 copy-start.6
  11.4 8.2 %copy-start.2 = (bf16[2,128,512]{2,1,0:T(8,128)(2,1)S(1)}, bf16[2,128,512]{2,1,0:T(8,128)(2,1)}, u32[]{:S(2)}) copy-start(bf16[2,128,512]{2,1,0:T(8,128)(2,1)} %param.17) | copy-start | bytes 786436
  59.3 99.0 %all-to-all-start = ((bf16[128,64,256]{2,1,0:T(8,128)(2,1)}), bf16[128,64,256]{2,1,0:T(8,128)(2,1)}, u32[]{:S(2)}, u32[]{:S(2)}) async-start(bf16[128,64,256]{2,1,0:T(8,128)(2,1)} %copy.86), calls=%async_computation | async-start | bytes 8388608 | tf_op jit(solution)/shard_map/all_to_all | solution.py:38
  158.3 97.6 %all-to-all-start.1 = ((bf16[128,64,256]{2,1,0:T(8,128)(2,1)}), bf16[128,64,256]{2,1,0:T(8,128)(2,1)}, u32[]{:S(2)}, u32[]{:S(2)}) async-start(bf16[128,64,256]{2,1,0:T(8,128)(2,1)} %copy.88), calls=%async_computation.1 | async-start | bytes 8388608 | tf_op jit(solution)/shard_map/all_to_all | solution.py:39
  287.3 11.7 %copy-start.7 = (f32[2,128]{1,0:T(2,128)S(1)}, f32[2,128]{1,0:T(2,128)}, u32[]{:S(2)}) copy-start(f32[2,128]{1,0:T(2,128)} %param.20) | copy-start | bytes 3076
  287.3 11.6 %copy-start.8 = (f32[2,128]{1,0:T(2,128)S(1)}, f32[2,128]{1,0:T(2,128)}, u32[]{:S(2)}) copy-start(f32[2,128]{1,0:T(2,128)} %param.19) | copy-start | bytes 3076
  294.0 97.4 %all-to-all-start.2 = ((bf16[8,1024,256]{2,0,1:T(8,128)(2,1)}), bf16[8,1024,256]{2,0,1:T(8,128)(2,1)}, u32[]{:S(2)}, u32[]{:S(2)}) async-start(bf16[8,1024,256]{2,0,1:T(8,128)(2,1)} %bitcast.138), calls=%async_computation.2 | async-start | bytes 8388608 | tf_op jit(solution)/shard_map/all_to_all | solution.py:54
  396.3 4.2 copy-start.3
  399.9 7.1 slice-start
  400.5 6.5 copy-start.9
  400.5 6.5 slice-start.1
  414.4 3.4 copy-start.1
  459.1 97.4 %all-to-all-start.3 = ((bf16[128,64,256]{2,1,0:T(8,128)(2,1)}), bf16[128,64,256]{2,1,0:T(8,128)(2,1)}, u32[]{:S(2)}, u32[]{:S(2)}) async-start(bf16[128,64,256]{2,1,0:T(8,128)(2,1)} %copy.101), calls=%async_computation.3 | async-start | bytes 8388608 | tf_op jit(solution)/shard_map/all_to_all | solution.py:38
  556.5 97.4 %all-to-all-start.4 = ((bf16[128,64,256]{2,1,0:T(8,128)(2,1)}), bf16[128,64,256]{2,1,0:T(8,128)(2,1)}, u32[]{:S(2)}, u32[]{:S(2)}) async-start(bf16[128,64,256]{2,1,0:T(8,128)(2,1)} %copy.103), calls=%async_computation.4 | async-start | bytes 8388608 | tf_op jit(solution)/shard_map/all_to_all | solution.py:39
  691.7 97.4 %all-to-all-start.5 = ((bf16[8,1024,256]{2,0,1:T(8,128)(2,1)}), bf16[8,1024,256]{2,0,1:T(8,128)(2,1)}, u32[]{:S(2)}, u32[]{:S(2)}) async-start(bf16[8,1024,256]{2,0,1:T(8,128)(2,1)} %bitcast.139), calls=%async_computation.5 | async-start | bytes 8388608 | tf_op jit(solution)/shard_map/all_to_all | solution.py:54
  797.5 3.8 slice-start.2
  798.1 3.2 slice-start.3
where the time goes:
time: 827 us; the launch traced here: 817 us
  waiting for transfers between devices  508 us (61%)
  local copies, waits for them, and re-layouts  151 us (18%)
  matrix products  73.3 us (9%)
  other arithmetic  51.2 us (6%)
  starting transfers between devices  31.4 us (4%)
    all_to_all x2, waiting for transfers between devices, triangle(): lax.all_to_all(packed, ('row', 'col'), split_axis=1, concat_axis=0, tiled...  184 us
    all_to_all x2, waiting for transfers between devices, triangle(): lax.all_to_all(left_side, ('row', 'col'), split_axis=0, concat_axis=1, ti...  171 us
    all_to_all x2, waiting for transfers between devices, triangle(): lax.all_to_all(right_side, ('row', 'col'), split_axis=0, concat_axis=1, t...  152 us
    dot_general x2, matrix products, body(): jnp.einsum('ijc,cf->fij', normed, proj[layer_index], preferred_element_ty...  34.6 us
    reshape x4, local copies, waits for them, and re-layouts, spread(): values.reshape(per_device, row_count, col_count, rows_here, cols_here)  34.3 us
    convert_element_type x2, other arithmetic, body(): right_side = (pair_mask * jax.nn.sigmoid(hidden_all[2 * hidden:3 * hidden...  30.7 us
    reshape x4, local copies, waits for them, and re-layouts, spread(): values.transpose(0, 1, 3, 2, 4)  30.6 us
  transfers between devices with their start and end apart: 6, of which 6 were waited for; matrix products, arithmetic and copies ran while one was open for 6% of the time, Pallas kernels for 0%

commit v1 on v0

v1 whole, which is shorter than its diff:
```python
import functools

import jax
import jax.numpy as jnp
from jax import lax
from jax.experimental import pallas as pl
from jax.experimental.pallas import tpu as pltpu
from jax.sharding import PartitionSpec as P

EPSILON = 1e-05
VMEM_LIMIT = 56 * 1024 * 1024


def norm(values, gain, bias, axis):
    center = values - jnp.mean(values, axis=axis, keepdims=True)
    variance = jnp.mean(center * center, axis=axis, keepdims=True)
    return center * lax.rsqrt(variance + EPSILON) * gain + bias


def dot(a, b, dims):
    return lax.dot_general(a, b, (dims, ((), ())), preferred_element_type=jnp.float32)


def project_row(row, normed, row_real, col_real, proj_t, left_rows, right_rows):
    hidden = left_rows.shape[1]
    mask = row_real * col_real
    both = dot(proj_t[...], normed, ((1,), (1,)))
    left = mask * jax.nn.sigmoid(both[:hidden]) * both[hidden : 2 * hidden]
    right = mask * jax.nn.sigmoid(both[2 * hidden : 3 * hidden]) * both[3 * hidden :]
    left_rows[row] = left.astype(jnp.bfloat16)
    right_rows[row] = right.astype(jnp.bfloat16)


def add_chain(pair_row, row_chain, col_chain, chain_term):
    same = (col_chain[...] == row_chain).astype(jnp.float32)
    return pair_row + same * chain_term[...]


def update_row(state, mixed, gain, bias, gate_w, hid_gain, hid_bias, out_w):
    normed = norm(state, gain, bias, -1).astype(jnp.bfloat16)
    gate = jax.nn.sigmoid(dot(normed, gate_w, ((1,), (0,))))
    normed_mix = norm(mixed.astype(jnp.float32), hid_gain, hid_bias, 0).astype(jnp.bfloat16)
    return state + gate * dot(normed_mix, out_w, ((0,), (0,)))


def first_kernel(
    chain_s, real_s, pair, col_chain, col_real, chain_term, gain, bias, proj_t,
    left, right, left_rows, right_rows,
):
    rows = pair.shape[0]
    base = pl.program_id(0) * rows

    @pl.loop(0, rows)
    def _(row):
        state = add_chain(pair[row], chain_s[base + row], col_chain, chain_term)
        normed = norm(state, gain[0:1], bias[0:1], -1).astype(jnp.bfloat16)
        project_row(row, normed, real_s[base + row], col_real[...], proj_t, left_rows, right_rows)

    left[...] = jnp.swapaxes(left_rows[...], 0, 1)
    right[...] = jnp.swapaxes(right_rows[...], 0, 1)


def middle_kernel(
    chain_s, real_s, pair, mixed, col_chain, col_real, chain_term, gain, bias, proj_t,
    gate_w, hid_gain, hid_bias, out_w,
    state_out, left, right, left_rows, right_rows, mixed_rows,
):
    rows = pair.shape[0]
    base = pl.program_id(0) * rows
    mixed_rows[...] = jnp.swapaxes(mixed[...], 0, 1)

    @pl.loop(0, rows)
    def _(row):
        state = add_chain(pair[row], chain_s[base + row], col_chain, chain_term)
        state = update_row(
            state, mixed_rows[row], gain[0:1], bias[0:1], gate_w[...], hid_gain[...],
            hid_bias[...], out_w[...],
        )
        state_out[row] = state
        normed = norm(state, gain[1:2], bias[1:2], -1).astype(jnp.bfloat16)
        project_row(row, normed, real_s[base + row], col_real[...], proj_t, left_rows, right_rows)

    left[...] = jnp.swapaxes(left_rows[...], 0, 1)
    right[...] = jnp.swapaxes(right_rows[...], 0, 1)


def last_kernel(
    state_in, mixed, gain, bias, gate_w, hid_gain, hid_bias, out_w, state_out, mixed_rows
):
    rows = state_in.shape[0]
    mixed_rows[...] = jnp.swapaxes(mixed[...], 0, 1)

    @pl.loop(0, rows)
    def _(row):
        state_out[row] = update_row(
            state_in[row], mixed_rows[row], gain[1:2], bias[1:2], gate_w[...], hid_gain[...],
            hid_bias[...], out_w[...],
        )


def triangle_kernel(outgoing, col_count, left, right, mixed):
    blocks, _, rows_here, cols_here = left.shape
    row_count = blocks // col_count
    tokens = row_count * rows_here

    def part(ref, c):
        value = ref[...].reshape(row_count, col_count, rows_here, cols_here)[:, c]
        return value.reshape(tokens, cols_here)

    if outgoing:
        total = None
        for c in range(col_count):
            term = dot(part(left, c), part(right, c), ((1,), (1,)))
            total = term if total is None else total + term
        total = total.astype(jnp.bfloat16)
        for c in range(col_count):
            piece = total[:, c * cols_here : (c + 1) * cols_here]
            piece = piece.reshape(row_count, rows_here, cols_here)
            for r in range(row_count):
                mixed[r * col_count + c, 0] = piece[r]
    else:
        for ci in range(col_count):
            for cj in range(col_count):
                total = dot(part(left, ci), part(right, cj), ((0,), (0,))).astype(jnp.bfloat16)
                span = cols_here // rows_here
                for r in range(span):
                    mixed[(ci * span + r) * col_count + cj, 0] = total[
                        r * rows_here : (r + 1) * rows_here
                    ]


def triangle(left, right, outgoing):
    hidden, rows_here, cols_here = left.shape
    row_count = lax.axis_size("row")
    col_count = lax.axis_size("col")
    blocks = row_count * col_count
    per_device = hidden // blocks
    recv = []
    for side in (left, right):
        side = side.reshape(blocks, per_device, rows_here, cols_here)
        recv.append(lax.all_to_all(side, ("row", "col"), 0, 0, tiled=True))
    spec = pl.BlockSpec((blocks, 1, rows_here, cols_here), lambda h: (0, h, 0, 0))
    mixed = pl.pallas_call(
        functools.partial(triangle_kernel, outgoing, col_count),
        grid=(per_device,),
        in_specs=[spec, spec],
        out_specs=spec,
        out_shape=jax.ShapeDtypeStruct(recv[0].shape, jnp.bfloat16),
        compiler_params=pltpu.CompilerParams(vmem_limit_bytes=VMEM_LIMIT),
        name="triangle_product",
    )(*recv)
    mixed = lax.all_to_all(mixed, ("row", "col"), 0, 0, tiled=True)
    return mixed.reshape(hidden, rows_here, cols_here)


def body(
    pair, token_count, chain_ids, chain_term, in_gain, in_bias, proj, gate_w, hid_gain,
    hid_bias, out_w,
):
    rows_here, cols_here, width = pair.shape
    hidden = proj.shape[2] // 4
    row_first = lax.axis_index("row") * rows_here
    col_first = lax.axis_index("col") * cols_here
    positions = jnp.arange(chain_ids.shape[0], dtype=jnp.int32)
    real = (positions < token_count[0]).astype(jnp.float32)
    row_real = lax.dynamic_slice_in_dim(real, row_first, rows_here, 0)
    col_real = lax.dynamic_slice_in_dim(real, col_first, cols_here, 0)[None, :]
    row_chain = lax.dynamic_slice_in_dim(chain_ids, row_first, rows_here, 0)
    col_chain = lax.dynamic_slice_in_dim(chain_ids, col_first, cols_here, 0)[:, None]
    chain_term = chain_term[None, :]
    proj_t = proj.transpose(0, 2, 1)
    hid_gain = hid_gain[:, :, None]
    hid_bias = hid_bias[:, :, None]

    tile = 16
    smem = pl.BlockSpec(memory_space=pltpu.SMEM)
    whole = pl.BlockSpec(memory_space=pltpu.VMEM)
    pixels = pl.BlockSpec((tile, cols_here, width), lambda i: (i, 0, 0))
    planes = pl.BlockSpec((hidden, tile, cols_here), lambda i: (0, i, 0))
    planes_shape = jax.ShapeDtypeStruct((hidden, rows_here, cols_here), jnp.bfloat16)
    pixels_shape = jax.ShapeDtypeStruct(pair.shape, jnp.float32)
    rows_scratch = pltpu.VMEM((tile, hidden, cols_here), jnp.bfloat16)
    grid = (rows_here // tile,)
    params = pltpu.CompilerParams(vmem_limit_bytes=VMEM_LIMIT)

    left, right = pl.pallas_call(
        first_kernel,
        grid=grid,
        in_specs=[smem, smem, pixels] + [whole] * 6,
        out_specs=[planes, planes],
        out_shape=[planes_shape, planes_shape],
        scratch_shapes=[rows_scratch] * 2,
        compiler_params=params,
        name="first_projection",
    )(row_chain, row_real, pair, col_chain, col_real, chain_term, in_gain, in_bias, proj_t[0])
    mixed = triangle(left, right, True)
    state, left, right = pl.pallas_call(
        middle_kernel,
        grid=grid,
        in_specs=[smem, smem, pixels, planes] + [whole] * 10,
        out_specs=[pixels, planes, planes],
        out_shape=[pixels_shape, planes_shape, planes_shape],
        scratch_shapes=[rows_scratch] * 3,
        compiler_params=params,
        name="update_and_projection",
    )(
        row_chain, row_real, pair, mixed, col_chain, col_real, chain_term, in_gain, in_bias,
        proj_t[1], gate_w[0], hid_gain[0], hid_bias[0], out_w[0],
    )
    mixed = triangle(left, right, False)
    return pl.pallas_call(
        last_kernel,
        grid=grid,
        in_specs=[pixels, planes] + [whole] * 6,
        out_specs=pixels,
        out_shape=pixels_shape,
        scratch_shapes=[rows_scratch],
        compiler_params=params,
        name="last_update",
    )(state, mixed, in_gain, in_bias, gate_w[1], hid_gain[1], hid_bias[1], out_w[1])


def solution(mesh):
    return jax.shard_map(
        body,
        mesh=mesh,
        in_specs=(P(("grp", "row"), "col", None), P("grp"), P("grp")) + (P(),) * 8,
        out_specs=P(("grp", "row"), "col", None),
        check_vma=False,
    )
```

time: 827 us -> 745 us (0.901); the launches traced: 817 us -> 744 us
  blocking collectives: 0 us -> 392 us
  waiting for transfers between devices: 508 us -> 181 us
  Pallas kernels: 0 us -> 150 us
  local copies, waits for them, and re-layouts: 151 us -> 9.63 us
  matrix products: 73.3 us -> 0 us
  other arithmetic: 51.2 us -> 0.01 us
  starting transfers between devices: 31.4 us -> 10.8 us
    all_to_all x0 -> x4, blocking collectives: none -> 392 us  [triangle(): recv.append(lax.all_to_all(side, ('row', 'col'), 0, 0, tiled=True))]
    all_to_all x6 -> x2, waiting for transfers between devices: 508 us -> 181 us  [triangle(): mixed = lax.all_to_all(mixed, ('row', 'col'), 0, 0, tiled=True)]
    pallas_call x0 -> x5, Pallas kernels: none -> 150 us  [the longest x1 66.1 us: body(): pl.pallas_call(middle_kernel, grid=grid, in_specs=[smem, smem, pixels, pl...]
    reshape x12 -> x0, local copies, waits for them, and re-layouts: 92.6 us -> none  [the longest x4 34.3 us: spread(): values.reshape(per_device, row_count, col_count, rows_here, cols_here)]
    dot_general x8 -> x0, matrix products: 73.3 us -> none  [the longest x2 34.6 us: body(): jnp.einsum('ijc,cf->fij', normed, proj[layer_index], preferred_element_ty...]
    convert_element_type x6 -> x1, other arithmetic: 38 us -> 0.01 us  [body(): real = (positions < token_count[0]).astype(jnp.float32)]
    convert_element_type x6 -> x0, local copies, waits for them, and re-layouts: 28.5 us -> none  [the longest x2 13.7 us: body(): left_side = (pair_mask * jax.nn.sigmoid(hidden_all[:hidden]) * hidden_all...]
    all_to_all x6 -> x2, starting transfers between devices: 31.4 us -> 10.8 us  [triangle(): mixed = lax.all_to_all(mixed, ('row', 'col'), 0, 0, tiled=True)]
  transfers between devices with their start and end apart: 6 -> 2, of which waited for: 6 -> 2; matrix products, arithmetic and copies ran while one was open for 6% -> 0% of each run, Pallas kernels for 0% -> 0%
where the time goes in v1:
time: 745 us; the launch traced here: 744 us
  blocking collectives  392 us (53%)
  waiting for transfers between devices  181 us (24%)
  Pallas kernels  150 us (20%)
  starting transfers between devices  10.8 us (1%)
  local copies, waits for them, and re-layouts  9.63 us (1%)
    all_to_all x4, blocking collectives, triangle(): recv.append(lax.all_to_all(side, ('row', 'col'), 0, 0, tiled=True))  392 us
    all_to_all x2, waiting for transfers between devices, triangle(): mixed = lax.all_to_all(mixed, ('row', 'col'), 0, 0, tiled=True)  181 us
    pallas_call x1, Pallas kernels, body(): pl.pallas_call(middle_kernel, grid=grid, in_specs=[smem, smem, pixels, pl...  66.1 us
    pallas_call x1, Pallas kernels, body(): pl.pallas_call(first_kernel, grid=grid, in_specs=[smem, smem, pixels] + [...  35.7 us
    pallas_call x1, Pallas kernels, body(): pl.pallas_call(last_kernel, grid=grid, in_specs=[pixels, planes] + [whole...  30.3 us
    pallas_call x2, Pallas kernels, triangle(): pl.pallas_call(functools.partial(triangle_kernel, outgoing, col_count), g...  17.9 us
  transfers between devices with their start and end apart: 2, of which 2 were waited for; matrix products, arithmetic and copies ran while one was open for 0% of the time, Pallas kernels for 0%

profile of v1, /device:TPU:13, one launch (start us, length us, event | category | flops | bytes accessed | tf_op | source)
XLA Modules:
  0.0 744.0 jit_solution(10246440193027538984)
XLA Ops:
  0.7 0.7 dynamic_slice.15
  1.3 0.6 dynamic_slice.13.real_s
  2.0 0.8 dynamic_slice.14
  2.7 1.3 dynamic_slice.12.chain_s
  4.0 0.8 copy.18.col_chain
  4.9 1.1 copy.17
  6.0 0.7 slice_bitcast_fusion
  6.7 35.7 %first_projection.1 = (bf16[128,64,256]{2,1,0:T(8,128)(2,1)}, bf16[128,64,256]{2,1,0:T(8,128)(2,1)}) custom-call(s32[64]{0:T(128)} %dynamic_slice.12.chain_s, f32[64]{0:T(128)} %dynamic_slice.13.real_s, f32[64,256,128]{2,1,0:T(8,128)} %pair.3, s32[256,1]{1,0:T(8,128)} %copy.18.col_chain, f32[1,256]{1,0:T(1,128)} %bitcast.37, f32[1,128]{1,0:T(1,128)} %bitcast.40, ...), custom_call_target="tpu_custom_call" | custom-call | tf_op jit(solution)/shard_map/first_projection/pallas_call | solution.py:186
  42.4 0.0 copy-start.1
  42.4 99.2 %all_to_all.30.left = bf16[16,8,64,256]{3,2,1,0:T(8,128)(2,1)} all-to-all(bf16[16,8,64,256]{3,2,1,0:T(8,128)(2,1)} %bitcast.35), channel_id=1, replica_groups=mesh['grp'=2,'row'=8,'col'=2] {'row','col'}, dimensions={0} | all-to-all | bytes 8388608 | tf_op jit(solution)/shard_map/all_to_all | solution.py:141
  141.6 0.0 copy-done.1
  141.6 97.5 %all_to_all.31.right = bf16[16,8,64,256]{3,2,1,0:T(8,128)(2,1)} all-to-all(bf16[16,8,64,256]{3,2,1,0:T(8,128)(2,1)S(1)} %bitcast.34), channel_id=1, replica_groups=mesh['grp'=2,'row'=8,'col'=2] {'row','col'}, dimensions={0} | all-to-all | bytes 8388608 | tf_op jit(solution)/shard_map/all_to_all | solution.py:141
  239.1 8.9 %triangle_product.2 = bf16[16,8,64,256]{3,2,1,0:T(8,128)(2,1)} custom-call(bf16[16,8,64,256]{3,2,1,0:T(8,128)(2,1)} %all_to_all.30.left, bf16[16,8,64,256]{3,2,1,0:T(8,128)(2,1)} %all_to_all.31.right), custom_call_target="tpu_custom_call" | custom-call | tf_op jit(solution)/shard_map/triangle_product/pallas_call | solution.py:143
  248.0 0.0 copy-start.4
  248.0 0.0 copy-start.5
  248.0 0.0 copy-start.2
  248.0 0.0 copy-start.3
  248.0 5.5 all-to-all-start.2
  253.5 0.0 copy-done.4
  253.5 0.7 copy.20.hid_gain
  254.2 0.0 copy-done.5
  254.2 0.7 copy.21.hid_bias
  254.9 0.0 copy-done.2
  254.9 0.0 copy-done.3
  254.9 0.7 slice_bitcast_fusion.2
  255.6 90.3 %all-to-all-done.2 = bf16[16,8,64,256]{3,2,1,0:T(8,128)(2,1)} async-done(((bf16[16,8,64,256]{3,2,1,0:T(8,128)(2,1)}), bf16[16,8,64,256]{3,2,1,0:T(8,128)(2,1)}, u32[]{:S(2)}, u32[]{:S(2)}) %all-to-all-start.2) | async-done | bytes 4194336 | tf_op jit(solution)/shard_map/all_to_all | solution.py:152
  345.9 66.1 %update_and_projection.1 = (f32[64,256,128]{2,1,0:T(8,128)}, bf16[128,64,256]{2,1,0:T(8,128)(2,1)}, bf16[128,64,256]{2,1,0:T(8,128)(2,1)}) custom-call(s32[64]{0:T(128)} %dynamic_slice.12.chain_s, f32[64]{0:T(128)} %dynamic_slice.13.real_s, f32[64,256,128]{2,1,0:T(8,128)} %pair.3, bf16[128,64,256]{2,1,0:T(8,128)(2,1)} %bitcast.8.mixed, ...), custom_call_target="tpu_custom_call" | custom-call | tf_op jit(solution)/shard_map/update_and_projection/pallas_call | solution.py:197
  412.0 0.0 copy-start
  412.0 97.5 %all_to_all.32.left = bf16[16,8,64,256]{3,2,1,0:T(8,128)(2,1)} all-to-all(bf16[16,8,64,256]{3,2,1,0:T(8,128)(2,1)} %bitcast.33), channel_id=1, replica_groups=mesh['grp'=2,'row'=8,'col'=2] {'row','col'}, dimensions={0} | all-to-all | bytes 8388608 | tf_op jit(solution)/shard_map/all_to_all | solution.py:141
  509.5 0.0 copy-done
  509.5 97.5 %all_to_all.33.right = bf16[16,8,64,256]{3,2,1,0:T(8,128)(2,1)} all-to-all(bf16[16,8,64,256]{3,2,1,0:T(8,128)(2,1)S(1)} %bitcast.32), channel_id=1, replica_groups=mesh['grp'=2,'row'=8,'col'=2] {'row','col'}, dimensions={0} | all-to-all | bytes 8388608 | tf_op jit(solution)/shard_map/all_to_all | solution.py:141
  606.9 9.0 %triangle_product.3 = bf16[16,8,64,256]{3,2,1,0:T(8,128)(2,1)} custom-call(bf16[16,8,64,256]{3,2,1,0:T(8,128)(2,1)} %all_to_all.32.left, bf16[16,8,64,256]{3,2,1,0:T(8,128)(2,1)} %all_to_all.33.right), custom_call_target="tpu_custom_call" | custom-call | tf_op jit(solution)/shard_map/triangle_product/pallas_call | solution.py:143
  615.9 5.3 all-to-all-start.5
  621.3 0.7 copy.22.hid_gain
  622.0 0.7 copy.23.hid_bias
  622.7 91.0 %all-to-all-done.5 = bf16[16,8,64,256]{3,2,1,0:T(8,128)(2,1)} async-done(((bf16[16,8,64,256]{3,2,1,0:T(8,128)(2,1)}), bf16[16,8,64,256]{3,2,1,0:T(8,128)(2,1)}, u32[]{:S(2)}, u32[]{:S(2)}) %all-to-all-start.5) | async-done | bytes 4194336 | tf_op jit(solution)/shard_map/all_to_all | solution.py:152
  713.7 30.3 %last_update.1 = f32[64,256,128]{2,1,0:T(8,128)} custom-call(f32[64,256,128]{2,1,0:T(8,128)} %get-tuple-element.12.state_in, bf16[128,64,256]{2,1,0:T(8,128)(2,1)} %bitcast.16.mixed, f32[2,128]{1,0:T(2,128)} %gain.5, f32[2,128]{1,0:T(2,128)} %bias.5, bf16[128,128]{1,0:T(8,128)(2,1)} %get-tuple-element.26.gate_w, f32[128,1]{1,0:T(8,128)} %copy.22.hid_gain, ...), custom_call_target="tpu_custom_call" | custom-call | tf_op jit(solution)/shard_map/last_update/pallas_call | solution.py:211
  (3 shorter events, 0.0 us)
Async XLA Ops:
  42.4 99.2 %copy-start.1 = (bf16[128,64,256]{2,1,0:T(8,128)(2,1)S(1)}, bf16[128,64,256]{2,1,0:T(8,128)(2,1)}, u32[]{:S(2)}) copy-start(bf16[128,64,256]{2,1,0:T(8,128)(2,1)} %get-tuple-element.11) | copy-start | bytes 12582916
  248.0 5.5 copy-start.4
  248.0 6.2 copy-start.5
  248.0 7.0 copy-start.2
  248.0 7.0 copy-start.3
  248.0 97.9 %all-to-all-start.2 = ((bf16[16,8,64,256]{3,2,1,0:T(8,128)(2,1)}), bf16[16,8,64,256]{3,2,1,0:T(8,128)(2,1)}, u32[]{:S(2)}, u32[]{:S(2)}) async-start(bf16[16,8,64,256]{3,2,1,0:T(8,128)(2,1)} %triangle_product.2), calls=%async_computation.2 | async-start | bytes 8388608 | tf_op jit(solution)/shard_map/all_to_all | solution.py:152
  412.0 97.5 %copy-start = (bf16[128,64,256]{2,1,0:T(8,128)(2,1)S(1)}, bf16[128,64,256]{2,1,0:T(8,128)(2,1)}, u32[]{:S(2)}) copy-start(bf16[128,64,256]{2,1,0:T(8,128)(2,1)} %get-tuple-element.14) | copy-start | bytes 12582916
  615.9 97.8 %all-to-all-start.5 = ((bf16[16,8,64,256]{3,2,1,0:T(8,128)(2,1)}), bf16[16,8,64,256]{3,2,1,0:T(8,128)(2,1)}, u32[]{:S(2)}, u32[]{:S(2)}) async-start(bf16[16,8,64,256]{3,2,1,0:T(8,128)(2,1)} %triangle_product.3), calls=%async_computation.5 | async-start | bytes 8388608 | tf_op jit(solution)/shard_map/all_to_all | solution.py:152

commit v2 on v1

--- a/solution.py
+++ b/solution.py
@@ -98,59 +98,194 @@
         )
 
 
-def triangle_kernel(outgoing, col_count, left, right, mixed):
-    blocks, _, rows_here, cols_here = left.shape
-    row_count = blocks // col_count
-    tokens = row_count * rows_here
-
-    def part(ref, c):
-        value = ref[...].reshape(row_count, col_count, rows_here, cols_here)[:, c]
-        return value.reshape(tokens, cols_here)
-
-    if outgoing:
-        total = None
-        for c in range(col_count):
-            term = dot(part(left, c), part(right, c), ((1,), (1,)))
-            total = term if total is None else total + term
-        total = total.astype(jnp.bfloat16)
-        for c in range(col_count):
-            piece = total[:, c * cols_here : (c + 1) * cols_here]
-            piece = piece.reshape(row_count, rows_here, cols_here)
-            for r in range(row_count):
-                mixed[r * col_count + c, 0] = piece[r]
-    else:
-        for ci in range(col_count):
-            for cj in range(col_count):
-                total = dot(part(left, ci), part(right, cj), ((0,), (0,))).astype(jnp.bfloat16)
-                span = cols_here // rows_here
-                for r in range(span):
-                    mixed[(ci * span + r) * col_count + cj, 0] = total[
-                        r * rows_here : (r + 1) * rows_here
-                    ]
+def triangle_kernel(
+    outgoing, groups, parts, left, right, mixed,
+    left_all, right_all, away, landed, result,
+    send_sem, side_sem, away_send, away_recv, back_send, back_recv,
+):
+    cols, per_device, half, cols_here = left_all.shape
+    rows_here = left.shape[1]
+    grp, row, col = lax.axis_index("grp"), lax.axis_index("row"), lax.axis_index("col")
+    inner = lax.axis_size("row") // 4
+    plane = row // inner
+    place = lax.rem(row, inner) * cols + col
+    is_middle = (plane == 1) | (plane == 2)
+    upper = plane // 2
+    middle = 1 + upper
+    chunk = per_device // parts
+
+    def device(to_plane, to_place):
+        return (grp, to_plane * inner + to_place // cols, lax.rem(to_place, cols))
+
+    def row_offset(at_plane, at_row):
+        return pl.multiple_of((lax.rem(at_plane, 2) * inner + at_row) * rows_here, rows_here)
+
+    me = row * cols + col
+    total = 4 * groups
+    barrier = pltpu.get_barrier_semaphore()
+
+    @pl.loop(1, total)
+    def _(step):
+        to = lax.rem(me + step, total)
+        pl.semaphore_signal(
+            barrier, inc=1, device_id=(grp, to // cols, lax.rem(to, cols)),
+            device_id_type=pl.DeviceIdType.MESH,
+        )
+
+    pl.semaphore_wait(barrier, total - 1)
+
+    my_offset = row_offset(plane, lax.rem(row, inner))
+
+    @pl.loop(0, parts)
+    def _(part):
+        order = ((right, right_all, 1), (left, left_all, 0))
+        for source, target, side in order:
+            for step in range(groups):
+                to = lax.rem(place + step, groups)
+                src = source.at[pl.ds(to * per_device + part * chunk, chunk)]
+                dst = target.at[col, pl.ds(part * chunk, chunk), pl.ds(my_offset, rows_here)]
+
+                def send(src=src, dst=dst, to=to, side=side):
+                    pltpu.make_async_remote_copy(
+                        src_ref=src, dst_ref=dst, send_sem=send_sem.at[side, part],
+                        recv_sem=side_sem.at[side, part], device_id=device(middle, to),
+                        device_id_type=pl.DeviceIdType.MESH,
+                    ).start()
+
+                def keep(src=src, dst=dst, side=side):
+                    pltpu.make_async_copy(src, dst, side_sem.at[side, part]).start()
+
+                if step == 0:
+                    pl.when(is_middle)(keep)
+                    pl.when(jnp.logical_not(is_middle))(send)
+                else:
+                    send()
+
+    def landed_side(ref, side, part):
+        span = ref.at[:, pl.ds(part * chunk, chunk)]
+        pltpu.make_async_copy(span, span, side_sem.at[side, part]).wait()
+
+    leaving = right_all if outgoing else away
+
+    def across(part):
+        span = pl.ds(part * chunk, chunk)
+        return pltpu.make_async_remote_copy(
+            src_ref=leaving.at[:, span], dst_ref=landed.at[:, span],
+            send_sem=away_send.at[part], recv_sem=away_recv.at[part],
+            device_id=device(3 - middle, place), device_id_type=pl.DeviceIdType.MESH,
+        )
+
+    def begin(part):
+        landed_side(right_all, 1, part)
+        if not outgoing:
+            landed_side(left_all, 0, part)
+
+            @pl.loop(0, chunk)
+            def _(index):
+                channel = part * chunk + index
+                ours = left_all[1 - upper, channel]
+                for c in range(cols):
+                    away[c, channel] = dot(
+                        ours, right_all[c, channel], ((0,), (0,))
+                    ).astype(jnp.bfloat16)
+
+        across(part).start()
+
+    def finish(part):
+        if outgoing:
+            landed_side(left_all, 0, part)
+        across(part).wait_recv()
+
+        @pl.loop(0, chunk)
+        def _(index):
+            channel = part * chunk + index
+            if outgoing:
+                for held, half_index in ((right_all, upper), (landed, 1 - upper)):
+                    value = dot(left_all[0, channel], held[0, channel], ((1,), (1,)))
+                    for c in range(1, cols):
+                        value += dot(left_all[c, channel], held[c, channel], ((1,), (1,)))
+                    result[half_index, channel] = value.astype(jnp.bfloat16)
+            else:
+                ours = left_all[upper, channel]
+                for c in range(cols):
+                    value = dot(ours, right_all[c, channel], ((0,), (0,)))
+                    value += landed[c, channel].astype(jnp.float32)
+                    result[c, channel] = value.astype(jnp.bfloat16)
+
+        for edge in (True, False):
+            to_plane = 3 * upper if edge else middle
+            for step in range(groups):
+                to = lax.rem(place + step, groups)
+                offset = row_offset(to_plane, to // cols)
+                src = result.at[
+                    lax.rem(to, cols), pl.ds(part * chunk, chunk), pl.ds(offset, rows_here)
+                ]
+                dst = mixed.at[pl.ds(place * per_device + part * chunk, chunk)]
+                if step == 0 and not edge:
+                    pltpu.make_async_copy(src, dst, back_recv).start()
+                else:
+                    pltpu.make_async_remote_copy(
+                        src_ref=src, dst_ref=dst, send_sem=back_send.at[part],
+                        recv_sem=back_recv, device_id=device(to_plane, to),
+                        device_id_type=pl.DeviceIdType.MESH,
+                    ).start()
+
+    @pl.when(is_middle)
+    def _():
+        begin(0)
+
+        @pl.loop(1, parts)
+        def _(part):
+            begin(part)
+            finish(part - 1)
+
+        finish(parts - 1)
+
+        @pl.loop(0, parts)
+        def _(part):
+            across(part).wait_send()
+            sent = mixed.at[pl.ds(0, (2 * groups - 1) * chunk)]
+            pltpu.make_async_copy(sent, sent, back_send.at[part]).wait()
+
+    @pl.loop(0, parts)
+    def _(part):
+        for side in range(2):
+            for condition, count in ((is_middle, groups - 1), (jnp.logical_not(is_middle), groups)):
+                @pl.when(condition)
+                def _(count=count, side=side):
+                    sent = left.at[pl.ds(0, count * chunk)]
+                    pltpu.make_async_copy(sent, sent, send_sem.at[side, part]).wait()
+
+    pltpu.make_async_copy(mixed, mixed, back_recv).wait()
 
 
 def triangle(left, right, outgoing):
     hidden, rows_here, cols_here = left.shape
     row_count = lax.axis_size("row")
     col_count = lax.axis_size("col")
-    blocks = row_count * col_count
-    per_device = hidden // blocks
-    recv = []
-    for side in (left, right):
-        side = side.reshape(blocks, per_device, rows_here, cols_here)
-        recv.append(lax.all_to_all(side, ("row", "col"), 0, 0, tiled=True))
-    spec = pl.BlockSpec((blocks, 1, rows_here, cols_here), lambda h: (0, h, 0, 0))
-    mixed = pl.pallas_call(
-        functools.partial(triangle_kernel, outgoing, col_count),
-        grid=(per_device,),
-        in_specs=[spec, spec],
-        out_specs=spec,
-        out_shape=jax.ShapeDtypeStruct(recv[0].shape, jnp.bfloat16),
-        compiler_params=pltpu.CompilerParams(vmem_limit_bytes=VMEM_LIMIT),
-        name="triangle_product",
-    )(*recv)
-    mixed = lax.all_to_all(mixed, ("row", "col"), 0, 0, tiled=True)
-    return mixed.reshape(hidden, rows_here, cols_here)
+    groups = row_count // 4 * col_count
+    per_device = hidden // groups
+    parts = min(8, per_device)
+    half = row_count // 2 * rows_here
+    held = pltpu.VMEM((col_count, per_device, half, cols_here), jnp.bfloat16)
+    small = pltpu.VMEM((16, 128), jnp.bfloat16)
+    anywhere = pl.BlockSpec(memory_space=pl.ANY)
+    sems = pltpu.SemaphoreType.DMA
+    return pl.pallas_call(
+        functools.partial(triangle_kernel, outgoing, groups, parts),
+        in_specs=[anywhere, anywhere],
+        out_specs=anywhere,
+        out_shape=jax.ShapeDtypeStruct(left.shape, jnp.bfloat16),
+        scratch_shapes=[
+            held, held, small if outgoing else held, held, held,
+            sems((2, parts)), sems((2, parts)), sems((parts,)), sems((parts,)), sems((parts,)), sems,
+        ],
+        compiler_params=pltpu.CompilerParams(
+            collective_id=1 if outgoing else 2, has_side_effects=True,
+            vmem_limit_bytes=VMEM_LIMIT,
+        ),
+        name="outgoing_product" if outgoing else "incoming_product",
+    )(left, right)
 
 
 def body(

time: 745 us -> 602 us (0.81)
  Pallas kernels: 150 us -> 591 us
  blocking collectives: 392 us -> 0 us
  waiting for transfers between devices: 181 us -> 0 us
  starting transfers between devices: 10.8 us -> 0 us
    pallas_call x2, Pallas kernels: 17.9 us -> 459 us  [triangle(): pl.pallas_call(functools.partial(triangle_kernel, outgoing, groups, parts...]
    all_to_all x4 -> x0, blocking collectives: 392 us -> none  [triangle(): recv.append(lax.all_to_all(side, ('row', 'col'), 0, 0, tiled=True))]
    all_to_all x2 -> x0, waiting for transfers between devices: 181 us -> none  [triangle(): mixed = lax.all_to_all(mixed, ('row', 'col'), 0, 0, tiled=True)]
    all_to_all x2 -> x0, starting transfers between devices: 10.8 us -> none  [triangle(): mixed = lax.all_to_all(mixed, ('row', 'col'), 0, 0, tiled=True)]
  transfers between devices with their start and end apart: 2 -> 0, of which waited for: 2 -> 0; matrix products, arithmetic and copies ran while one was open for 0% -> 0% of each run, Pallas kernels for 0% -> 0%
where the time goes in v2:
time: 602 us; the launch traced here: 601 us
  Pallas kernels  591 us (98%)
  local copies, waits for them, and re-layouts  9.51 us (2%)
    pallas_call x2, Pallas kernels, triangle(): pl.pallas_call(functools.partial(triangle_kernel, outgoing, groups, parts...  459 us
    pallas_call x1, Pallas kernels, body(): pl.pallas_call(middle_kernel, grid=grid, in_specs=[smem, smem, pixels, pl...  66.1 us
    pallas_call x1, Pallas kernels, body(): pl.pallas_call(first_kernel, grid=grid, in_specs=[smem, smem, pixels] + [...  35.8 us
    pallas_call x1, Pallas kernels, body(): pl.pallas_call(last_kernel, grid=grid, in_specs=[pixels, planes] + [whole...  30.3 us

profile of v2, /device:TPU:13, one launch (start us, length us, event | category | flops | bytes accessed | tf_op | source)
XLA Modules:
  0.0 601.4 jit_solution(8304143175831724482)
XLA Ops:
  0.7 0.6 dynamic_slice.15
  1.3 0.6 dynamic_slice.13.real_s
  1.9 0.8 dynamic_slice.14
  2.6 0.8 copy.18.col_chain
  3.4 1.3 dynamic_slice.12.chain_s
  4.7 1.1 copy.17
  5.8 0.7 slice_bitcast_fusion
  6.6 35.8 %first_projection.1 = (bf16[128,64,256]{2,1,0:T(8,128)(2,1)}, bf16[128,64,256]{2,1,0:T(8,128)(2,1)}) custom-call(s32[64]{0:T(128)} %dynamic_slice.12.chain_s, f32[64]{0:T(128)} %dynamic_slice.13.real_s, f32[64,256,128]{2,1,0:T(8,128)} %pair.3, s32[256,1]{1,0:T(8,128)} %copy.18.col_chain, f32[1,256]{1,0:T(1,128)} %bitcast.27, f32[1,128]{1,0:T(1,128)} %bitcast.30, ...), custom_call_target="tpu_custom_call" | custom-call | tf_op jit(solution)/shard_map/first_projection/pallas_call | solution.py:321
  42.3 0.0 copy-start
  42.3 0.0 copy-start.1
  42.4 0.0 copy-start.2
  42.4 0.0 copy-start.3
  42.4 230.7 %outgoing_product.1.mixed = bf16[128,64,256]{2,1,0:T(8,128)(2,1)} custom-call(bf16[128,64,256]{2,1,0:T(8,128)(2,1)} %get-tuple-element.10.left, bf16[128,64,256]{2,1,0:T(8,128)(2,1)} %get-tuple-element.11.right), custom_call_target="tpu_custom_call" | custom-call | tf_op jit(solution)/shard_map/outgoing_product/pallas_call | solution.py:274
  273.1 0.0 copy-done
  273.1 0.0 copy-done.1
  273.1 0.7 slice_bitcast_fusion.2
  273.8 0.0 copy-done.2
  273.8 0.7 copy.20.hid_gain
  274.6 0.0 copy-done.3
  274.6 0.7 copy.21.hid_bias
  275.3 66.1 %update_and_projection.1 = (f32[64,256,128]{2,1,0:T(8,128)}, bf16[128,64,256]{2,1,0:T(8,128)(2,1)}, bf16[128,64,256]{2,1,0:T(8,128)(2,1)}) custom-call(s32[64]{0:T(128)} %dynamic_slice.12.chain_s, f32[64]{0:T(128)} %dynamic_slice.13.real_s, f32[64,256,128]{2,1,0:T(8,128)} %pair.3, bf16[128,64,256]{2,1,0:T(8,128)(2,1)} %outgoing_product.1.mixed, ...), custom_call_target="tpu_custom_call" | custom-call | tf_op jit(solution)/shard_map/update_and_projection/pallas_call | solution.py:332
  341.4 228.3 %incoming_product.1.mixed = bf16[128,64,256]{2,1,0:T(8,128)(2,1)} custom-call(bf16[128,64,256]{2,1,0:T(8,128)(2,1)} %get-tuple-element.13.left, bf16[128,64,256]{2,1,0:T(8,128)(2,1)} %get-tuple-element.14.right), custom_call_target="tpu_custom_call" | custom-call | tf_op jit(solution)/shard_map/incoming_product/pallas_call | solution.py:274
  569.7 0.7 copy.22.hid_gain
  570.4 0.7 copy.23.hid_bias
  571.1 30.3 %last_update.1 = f32[64,256,128]{2,1,0:T(8,128)} custom-call(f32[64,256,128]{2,1,0:T(8,128)} %get-tuple-element.12.state_in, bf16[128,64,256]{2,1,0:T(8,128)(2,1)} %incoming_product.1.mixed, f32[2,128]{1,0:T(2,128)} %gain.5, f32[2,128]{1,0:T(2,128)} %bias.5, bf16[128,128]{1,0:T(8,128)(2,1)} %get-tuple-element.26.gate_w, f32[128,1]{1,0:T(8,128)} %copy.22.hid_gain, ...), custom_call_target="tpu_custom_call" | custom-call | tf_op jit(solution)/shard_map/last_update/pallas_call | solution.py:346
  (3 shorter events, 0.0 us)
Async XLA Ops:
  42.3 230.8 %copy-start = (bf16[2,128,128]{2,1,0:T(8,128)(2,1)S(1)}, bf16[2,128,128]{2,1,0:T(8,128)(2,1)}, u32[]{:S(2)}) copy-start(bf16[2,128,128]{2,1,0:T(8,128)(2,1)} %param.21) | copy-start | bytes 196612
  42.3 230.8 %copy-start.1 = (bf16[2,128,128]{2,1,0:T(8,128)(2,1)S(1)}, bf16[2,128,128]{2,1,0:T(8,128)(2,1)}, u32[]{:S(2)}) copy-start(bf16[2,128,128]{2,1,0:T(8,128)(2,1)} %param.18) | copy-start | bytes 196612
  42.4 231.5 %copy-start.2 = (f32[2,128]{1,0:T(2,128)S(1)}, f32[2,128]{1,0:T(2,128)}, u32[]{:S(2)}) copy-start(f32[2,128]{1,0:T(2,128)} %param.19) | copy-start | bytes 3076
  42.4 232.2 %copy-start.3 = (f32[2,128]{1,0:T(2,128)S(1)}, f32[2,128]{1,0:T(2,128)}, u32[]{:S(2)}) copy-start(f32[2,128]{1,0:T(2,128)} %param.20) | copy-start | bytes 3076

commit v3 on v2

--- a/solution.py
+++ b/solution.py
@@ -17,6 +17,10 @@
     return center * lax.rsqrt(variance + EPSILON) * gain + bias
 
 
+def sigmoid(values):
+    return 0.5 + 0.5 * jnp.tanh(0.5 * values)
+
+
 def dot(a, b, dims):
     return lax.dot_general(a, b, (dims, ((), ())), preferred_element_type=jnp.float32)
 
@@ -25,8 +29,8 @@
     hidden = left_rows.shape[1]
     mask = row_real * col_real
     both = dot(proj_t[...], normed, ((1,), (1,)))
-    left = mask * jax.nn.sigmoid(both[:hidden]) * both[hidden : 2 * hidden]
-    right = mask * jax.nn.sigmoid(both[2 * hidden : 3 * hidden]) * both[3 * hidden :]
+    left = mask * sigmoid(both[:hidden]) * both[hidden : 2 * hidden]
+    right = mask * sigmoid(both[2 * hidden : 3 * hidden]) * both[3 * hidden :]
     left_rows[row] = left.astype(jnp.bfloat16)
     right_rows[row] = right.astype(jnp.bfloat16)
 
@@ -38,7 +42,7 @@
 
 def update_row(state, mixed, gain, bias, gate_w, hid_gain, hid_bias, out_w):
     normed = norm(state, gain, bias, -1).astype(jnp.bfloat16)
-    gate = jax.nn.sigmoid(dot(normed, gate_w, ((1,), (0,))))
+    gate = sigmoid(dot(normed, gate_w, ((1,), (0,))))
     normed_mix = norm(mixed.astype(jnp.float32), hid_gain, hid_bias, 0).astype(jnp.bfloat16)
     return state + gate * dot(normed_mix, out_w, ((0,), (0,)))
 
@@ -50,7 +54,7 @@
     rows = pair.shape[0]
     base = pl.program_id(0) * rows
 
-    @pl.loop(0, rows)
+    @pl.loop(0, rows, unroll=4)
     def _(row):
         state = add_chain(pair[row], chain_s[base + row], col_chain, chain_term)
         normed = norm(state, gain[0:1], bias[0:1], -1).astype(jnp.bfloat16)
@@ -69,7 +73,7 @@
     base = pl.program_id(0) * rows
     mixed_rows[...] = jnp.swapaxes(mixed[...], 0, 1)
 
-    @pl.loop(0, rows)
+    @pl.loop(0, rows, unroll=4)
     def _(row):
         state = add_chain(pair[row], chain_s[base + row], col_chain, chain_term)
         state = update_row(
@@ -90,7 +94,7 @@
     rows = state_in.shape[0]
     mixed_rows[...] = jnp.swapaxes(mixed[...], 0, 1)
 
-    @pl.loop(0, rows)
+    @pl.loop(0, rows, unroll=4)
     def _(row):
         state_out[row] = update_row(
             state_in[row], mixed_rows[row], gain[1:2], bias[1:2], gate_w[...], hid_gain[...],
@@ -265,7 +269,7 @@
     col_count = lax.axis_size("col")
     groups = row_count // 4 * col_count
     per_device = hidden // groups
-    parts = min(8, per_device)
+    parts = min(16, per_device)
     half = row_count // 2 * rows_here
     held = pltpu.VMEM((col_count, per_device, half, cols_here), jnp.bfloat16)
     small = pltpu.VMEM((16, 128), jnp.bfloat16)

time: 602 us -> 552 us (0.917)
  Pallas kernels: 591 us -> 541 us
    pallas_call x1, Pallas kernels: 66.1 us -> 39.2 us  [body(): pl.pallas_call(middle_kernel, grid=grid, in_specs=[smem, smem, pixels, pl...]
    pallas_call x1, Pallas kernels: 35.8 us -> 19.5 us  [body(): pl.pallas_call(first_kernel, grid=grid, in_specs=[smem, smem, pixels] + [...]
    pallas_call x1, Pallas kernels: 30.3 us -> 22.3 us  [body(): pl.pallas_call(last_kernel, grid=grid, in_specs=[pixels, planes] + [whole...]
where the time goes in v3:
time: 552 us; the launch traced here: 551 us
  Pallas kernels  541 us (98%)
  local copies, waits for them, and re-layouts  9.51 us (2%)
    pallas_call x2, Pallas kernels, triangle(): pl.pallas_call(functools.partial(triangle_kernel, outgoing, groups, parts...  460 us
    pallas_call x1, Pallas kernels, body(): pl.pallas_call(middle_kernel, grid=grid, in_specs=[smem, smem, pixels, pl...  39.2 us
    pallas_call x1, Pallas kernels, body(): pl.pallas_call(last_kernel, grid=grid, in_specs=[pixels, planes] + [whole...  22.3 us
    pallas_call x1, Pallas kernels, body(): pl.pallas_call(first_kernel, grid=grid, in_specs=[smem, smem, pixels] + [...  19.5 us

profile of v3, /device:TPU:13, one launch (start us, length us, event | category | flops | bytes accessed | tf_op | source)
XLA Modules:
  0.0 551.4 jit_solution(4407504424182410681)
XLA Ops:
  0.7 0.6 dynamic_slice.15
  1.3 0.6 dynamic_slice.13.real_s
  1.9 0.8 dynamic_slice.14
  2.6 0.8 copy.18.col_chain
  3.4 1.3 dynamic_slice.12.chain_s
  4.7 1.1 copy.17
  5.8 0.7 slice_bitcast_fusion
  6.6 19.5 %first_projection.1 = (bf16[128,64,256]{2,1,0:T(8,128)(2,1)}, bf16[128,64,256]{2,1,0:T(8,128)(2,1)}) custom-call(s32[64]{0:T(128)} %dynamic_slice.12.chain_s, f32[64]{0:T(128)} %dynamic_slice.13.real_s, f32[64,256,128]{2,1,0:T(8,128)} %pair.3, s32[256,1]{1,0:T(8,128)} %copy.18.col_chain, f32[1,256]{1,0:T(1,128)} %bitcast.27, f32[1,128]{1,0:T(1,128)} %bitcast.30, ...), custom_call_target="tpu_custom_call" | custom-call | tf_op jit(solution)/shard_map/first_projection/pallas_call | solution.py:325
  26.1 0.0 copy-start
  26.1 0.0 copy-start.1
  26.1 0.0 copy-start.2
  26.1 0.0 copy-start.3
  26.1 231.2 %outgoing_product.1.mixed = bf16[128,64,256]{2,1,0:T(8,128)(2,1)} custom-call(bf16[128,64,256]{2,1,0:T(8,128)(2,1)} %get-tuple-element.10.left, bf16[128,64,256]{2,1,0:T(8,128)(2,1)} %get-tuple-element.11.right), custom_call_target="tpu_custom_call" | custom-call | tf_op jit(solution)/shard_map/outgoing_product/pallas_call | solution.py:278
  257.4 0.0 copy-done
  257.4 0.0 copy-done.1
  257.4 0.7 slice_bitcast_fusion.2
  258.1 0.0 copy-done.2
  258.1 0.7 copy.20.hid_gain
  258.8 0.0 copy-done.3
  258.8 0.7 copy.21.hid_bias
  259.5 39.2 %update_and_projection.1 = (f32[64,256,128]{2,1,0:T(8,128)}, bf16[128,64,256]{2,1,0:T(8,128)(2,1)}, bf16[128,64,256]{2,1,0:T(8,128)(2,1)}) custom-call(s32[64]{0:T(128)} %dynamic_slice.12.chain_s, f32[64]{0:T(128)} %dynamic_slice.13.real_s, f32[64,256,128]{2,1,0:T(8,128)} %pair.3, bf16[128,64,256]{2,1,0:T(8,128)(2,1)} %outgoing_product.1.mixed, ...), custom_call_target="tpu_custom_call" | custom-call | tf_op jit(solution)/shard_map/update_and_projection/pallas_call | solution.py:336
  298.8 228.8 %incoming_product.1.mixed = bf16[128,64,256]{2,1,0:T(8,128)(2,1)} custom-call(bf16[128,64,256]{2,1,0:T(8,128)(2,1)} %get-tuple-element.13.left, bf16[128,64,256]{2,1,0:T(8,128)(2,1)} %get-tuple-element.14.right), custom_call_target="tpu_custom_call" | custom-call | tf_op jit(solution)/shard_map/incoming_product/pallas_call | solution.py:278
  527.6 0.7 copy.22.hid_gain
  528.3 0.7 copy.23.hid_bias
  529.1 22.3 %last_update.1 = f32[64,256,128]{2,1,0:T(8,128)} custom-call(f32[64,256,128]{2,1,0:T(8,128)} %get-tuple-element.12.state_in, bf16[128,64,256]{2,1,0:T(8,128)(2,1)} %incoming_product.1.mixed, f32[2,128]{1,0:T(2,128)} %gain.5, f32[2,128]{1,0:T(2,128)} %bias.5, bf16[128,128]{1,0:T(8,128)(2,1)} %get-tuple-element.26.gate_w, f32[128,1]{1,0:T(8,128)} %copy.22.hid_gain, ...), custom_call_target="tpu_custom_call" | custom-call | tf_op jit(solution)/shard_map/last_update/pallas_call | solution.py:350
  (3 shorter events, 0.0 us)
Async XLA Ops:
  26.1 231.3 %copy-start = (bf16[2,128,128]{2,1,0:T(8,128)(2,1)S(1)}, bf16[2,128,128]{2,1,0:T(8,128)(2,1)}, u32[]{:S(2)}) copy-start(bf16[2,128,128]{2,1,0:T(8,128)(2,1)} %param.21) | copy-start | bytes 196612
  26.1 231.3 %copy-start.1 = (bf16[2,128,128]{2,1,0:T(8,128)(2,1)S(1)}, bf16[2,128,128]{2,1,0:T(8,128)(2,1)}, u32[]{:S(2)}) copy-start(bf16[2,128,128]{2,1,0:T(8,128)(2,1)} %param.18) | copy-start | bytes 196612
  26.1 232.0 %copy-start.2 = (f32[2,128]{1,0:T(2,128)S(1)}, f32[2,128]{1,0:T(2,128)}, u32[]{:S(2)}) copy-start(f32[2,128]{1,0:T(2,128)} %param.19) | copy-start | bytes 3076
  26.1 232.7 %copy-start.3 = (f32[2,128]{1,0:T(2,128)S(1)}, f32[2,128]{1,0:T(2,128)}, u32[]{:S(2)}) copy-start(f32[2,128]{1,0:T(2,128)} %param.20) | copy-start | bytes 3076

commit v4 on v3

--- a/solution.py
+++ b/solution.py
@@ -54,7 +54,7 @@
     rows = pair.shape[0]
     base = pl.program_id(0) * rows
 
-    @pl.loop(0, rows, unroll=4)
+    @pl.loop(0, rows, unroll=8)
     def _(row):
         state = add_chain(pair[row], chain_s[base + row], col_chain, chain_term)
         normed = norm(state, gain[0:1], bias[0:1], -1).astype(jnp.bfloat16)
@@ -73,7 +73,7 @@
     base = pl.program_id(0) * rows
     mixed_rows[...] = jnp.swapaxes(mixed[...], 0, 1)
 
-    @pl.loop(0, rows, unroll=4)
+    @pl.loop(0, rows, unroll=8)
     def _(row):
         state = add_chain(pair[row], chain_s[base + row], col_chain, chain_term)
         state = update_row(
@@ -94,7 +94,7 @@
     rows = state_in.shape[0]
     mixed_rows[...] = jnp.swapaxes(mixed[...], 0, 1)
 
-    @pl.loop(0, rows, unroll=4)
+    @pl.loop(0, rows, unroll=8)
     def _(row):
         state_out[row] = update_row(
             state_in[row], mixed_rows[row], gain[1:2], bias[1:2], gate_w[...], hid_gain[...],
@@ -105,7 +105,7 @@
 def triangle_kernel(
     outgoing, groups, parts, left, right, mixed,
     left_all, right_all, away, landed, result,
-    send_sem, side_sem, away_send, away_recv, back_send, back_recv,
+    send_sem, side_sem, edge_send, away_send, away_recv, back_send, back_recv,
 ):
     cols, per_device, half, cols_here = left_all.shape
     rows_here = left.shape[1]
@@ -152,7 +152,7 @@
                 def send(src=src, dst=dst, to=to, side=side):
                     pltpu.make_async_remote_copy(
                         src_ref=src, dst_ref=dst, send_sem=send_sem.at[side, part],
-                        recv_sem=side_sem.at[side, part], device_id=device(middle, to),
+                        recv_sem=side_sem.at[side, part], device_id=device(plane, to),
                         device_id_type=pl.DeviceIdType.MESH,
                     ).start()
 
@@ -160,14 +160,34 @@
                     pltpu.make_async_copy(src, dst, side_sem.at[side, part]).start()
 
                 if step == 0:
-                    pl.when(is_middle)(keep)
-                    pl.when(jnp.logical_not(is_middle))(send)
+                    keep()
                 else:
                     send()
 
     def landed_side(ref, side, part):
         span = ref.at[:, pl.ds(part * chunk, chunk)]
         pltpu.make_async_copy(span, span, side_sem.at[side, part]).wait()
+
+    plane_rows = pl.ds(
+        pl.multiple_of(lax.rem(plane, 2) * inner * rows_here, rows_here), inner * rows_here
+    )
+
+    def forward(ref, side, part):
+        span = ref.at[:, pl.ds(part * chunk, chunk), plane_rows]
+        return pltpu.make_async_remote_copy(
+            src_ref=span, dst_ref=span, send_sem=edge_send.at[side, part],
+            recv_sem=side_sem.at[side, part], device_id=device(middle, place),
+            device_id_type=pl.DeviceIdType.MESH,
+        )
+
+    @pl.when(jnp.logical_not(is_middle))
+    def _():
+        @pl.loop(0, parts)
+        def _(part):
+            for ref, side in ((right_all, 1), (left_all, 0)):
+                span = ref.at[:, pl.ds(part * chunk, chunk), plane_rows]
+                pltpu.make_async_copy(span, span, side_sem.at[side, part]).wait()
+                forward(ref, side, part).start()
 
     leaving = right_all if outgoing else away
 
@@ -254,11 +274,15 @@
     @pl.loop(0, parts)
     def _(part):
         for side in range(2):
-            for condition, count in ((is_middle, groups - 1), (jnp.logical_not(is_middle), groups)):
-                @pl.when(condition)
-                def _(count=count, side=side):
-                    sent = left.at[pl.ds(0, count * chunk)]
-                    pltpu.make_async_copy(sent, sent, send_sem.at[side, part]).wait()
+            sent = left.at[pl.ds(0, (groups - 1) * chunk)]
+            pltpu.make_async_copy(sent, sent, send_sem.at[side, part]).wait()
+
+    @pl.when(jnp.logical_not(is_middle))
+    def _():
+        @pl.loop(0, parts)
+        def _(part):
+            for ref, side in ((right_all, 1), (left_all, 0)):
+                forward(ref, side, part).wait_send()
 
     pltpu.make_async_copy(mixed, mixed, back_recv).wait()
 
@@ -282,7 +306,7 @@
         out_shape=jax.ShapeDtypeStruct(left.shape, jnp.bfloat16),
         scratch_shapes=[
             held, held, small if outgoing else held, held, held,
-            sems((2, parts)), sems((2, parts)), sems((parts,)), sems((parts,)), sems((parts,)), sems,
+            sems((2, parts)), sems((2, parts)), sems((2, parts)), sems((parts,)), sems((parts,)), sems((parts,)), sems,
         ],
         compiler_params=pltpu.CompilerParams(
             collective_id=1 if outgoing else 2, has_side_effects=True,

time: 552 us -> 508 us (0.920)
  Pallas kernels: 541 us -> 494 us
    pallas_call x2, Pallas kernels: 460 us -> 416 us  [triangle(): pl.pallas_call(functools.partial(triangle_kernel, outgoing, groups, parts...]
where the time goes in v4:
time: 508 us; the launch traced here: 504 us
  Pallas kernels  494 us (97%)
  local copies, waits for them, and re-layouts  9.51 us (2%)
    pallas_call x2, Pallas kernels, triangle(): pl.pallas_call(functools.partial(triangle_kernel, outgoing, groups, parts...  416 us
    pallas_call x1, Pallas kernels, body(): pl.pallas_call(middle_kernel, grid=grid, in_specs=[smem, smem, pixels, pl...  38.2 us
    pallas_call x1, Pallas kernels, body(): pl.pallas_call(last_kernel, grid=grid, in_specs=[pixels, planes] + [whole...  20.9 us
    pallas_call x1, Pallas kernels, body(): pl.pallas_call(first_kernel, grid=grid, in_specs=[smem, smem, pixels] + [...  19.1 us

profile of v4, /device:TPU:13, one launch (start us, length us, event | category | flops | bytes accessed | tf_op | source)
XLA Modules:
  0.0 504.0 jit_solution(8353720343801754973)
XLA Ops:
  0.7 0.6 dynamic_slice.15
  1.3 0.6 dynamic_slice.13.real_s
  1.9 0.8 dynamic_slice.14
  2.6 0.8 copy.18.col_chain
  3.4 1.3 dynamic_slice.12.chain_s
  4.7 1.1 copy.17
  5.8 0.7 slice_bitcast_fusion
  6.6 19.1 %first_projection.1 = (bf16[128,64,256]{2,1,0:T(8,128)(2,1)}, bf16[128,64,256]{2,1,0:T(8,128)(2,1)}) custom-call(s32[64]{0:T(128)} %dynamic_slice.12.chain_s, f32[64]{0:T(128)} %dynamic_slice.13.real_s, f32[64,256,128]{2,1,0:T(8,128)} %pair.3, s32[256,1]{1,0:T(8,128)} %copy.18.col_chain, f32[1,256]{1,0:T(1,128)} %bitcast.27, f32[1,128]{1,0:T(1,128)} %bitcast.30, ...), custom_call_target="tpu_custom_call" | custom-call | tf_op jit(solution)/shard_map/first_projection/pallas_call | solution.py:349
  25.6 0.0 copy-start
  25.6 0.0 copy-start.1
  25.6 0.0 copy-start.2
  25.7 0.0 copy-start.3
  25.7 204.3 %outgoing_product.1.mixed = bf16[128,64,256]{2,1,0:T(8,128)(2,1)} custom-call(bf16[128,64,256]{2,1,0:T(8,128)(2,1)} %get-tuple-element.10.left, bf16[128,64,256]{2,1,0:T(8,128)(2,1)} %get-tuple-element.11.right), custom_call_target="tpu_custom_call" | custom-call | tf_op jit(solution)/shard_map/outgoing_product/pallas_call | solution.py:302
  230.0 0.0 copy-done
  230.0 0.0 copy-done.1
  230.0 0.7 slice_bitcast_fusion.2
  230.6 0.0 copy-done.2
  230.7 0.7 copy.20.hid_gain
  231.4 0.0 copy-done.3
  231.4 0.7 copy.21.hid_bias
  232.1 38.2 %update_and_projection.1 = (f32[64,256,128]{2,1,0:T(8,128)}, bf16[128,64,256]{2,1,0:T(8,128)(2,1)}, bf16[128,64,256]{2,1,0:T(8,128)(2,1)}) custom-call(s32[64]{0:T(128)} %dynamic_slice.12.chain_s, f32[64]{0:T(128)} %dynamic_slice.13.real_s, f32[64,256,128]{2,1,0:T(8,128)} %pair.3, bf16[128,64,256]{2,1,0:T(8,128)(2,1)} %outgoing_product.1.mixed, ...), custom_call_target="tpu_custom_call" | custom-call | tf_op jit(solution)/shard_map/update_and_projection/pallas_call | solution.py:360
  270.3 211.3 %incoming_product.1.mixed = bf16[128,64,256]{2,1,0:T(8,128)(2,1)} custom-call(bf16[128,64,256]{2,1,0:T(8,128)(2,1)} %get-tuple-element.13.left, bf16[128,64,256]{2,1,0:T(8,128)(2,1)} %get-tuple-element.14.right), custom_call_target="tpu_custom_call" | custom-call | tf_op jit(solution)/shard_map/incoming_product/pallas_call | solution.py:302
  481.6 0.7 copy.22.hid_gain
  482.4 0.7 copy.23.hid_bias
  483.1 20.9 %last_update.1 = f32[64,256,128]{2,1,0:T(8,128)} custom-call(f32[64,256,128]{2,1,0:T(8,128)} %get-tuple-element.12.state_in, bf16[128,64,256]{2,1,0:T(8,128)(2,1)} %incoming_product.1.mixed, f32[2,128]{1,0:T(2,128)} %gain.5, f32[2,128]{1,0:T(2,128)} %bias.5, bf16[128,128]{1,0:T(8,128)(2,1)} %get-tuple-element.26.gate_w, f32[128,1]{1,0:T(8,128)} %copy.22.hid_gain, ...), custom_call_target="tpu_custom_call" | custom-call | tf_op jit(solution)/shard_map/last_update/pallas_call | solution.py:374
  (3 shorter events, 0.0 us)
Async XLA Ops:
  25.6 204.3 %copy-start = (bf16[2,128,128]{2,1,0:T(8,128)(2,1)S(1)}, bf16[2,128,128]{2,1,0:T(8,128)(2,1)}, u32[]{:S(2)}) copy-start(bf16[2,128,128]{2,1,0:T(8,128)(2,1)} %param.21) | copy-start | bytes 196612
  25.6 204.3 %copy-start.1 = (bf16[2,128,128]{2,1,0:T(8,128)(2,1)S(1)}, bf16[2,128,128]{2,1,0:T(8,128)(2,1)}, u32[]{:S(2)}) copy-start(bf16[2,128,128]{2,1,0:T(8,128)(2,1)} %param.18) | copy-start | bytes 196612
  25.6 205.0 %copy-start.2 = (f32[2,128]{1,0:T(2,128)S(1)}, f32[2,128]{1,0:T(2,128)}, u32[]{:S(2)}) copy-start(f32[2,128]{1,0:T(2,128)} %param.19) | copy-start | bytes 3076
  25.7 205.7 %copy-start.3 = (f32[2,128]{1,0:T(2,128)S(1)}, f32[2,128]{1,0:T(2,128)}, u32[]{:S(2)}) copy-start(f32[2,128]{1,0:T(2,128)} %param.20) | copy-start | bytes 3076

commit v5 on v4

--- a/solution.py
+++ b/solution.py
@@ -293,7 +293,7 @@
     col_count = lax.axis_size("col")
     groups = row_count // 4 * col_count
     per_device = hidden // groups
-    parts = min(16, per_device)
+    parts = min(32, per_device)
     half = row_count // 2 * rows_here
     held = pltpu.VMEM((col_count, per_device, half, cols_here), jnp.bfloat16)
     small = pltpu.VMEM((16, 128), jnp.bfloat16)

time: 508 us -> 494 us (0.972)
  Pallas kernels: 494 us -> 480 us
    pallas_call x2, Pallas kernels: 416 us -> 402 us  [triangle(): pl.pallas_call(functools.partial(triangle_kernel, outgoing, groups, parts...]
where the time goes in v5:
time: 494 us; the launch traced here: 491 us
  Pallas kernels  480 us (97%)
  local copies, waits for them, and re-layouts  9.51 us (2%)
    pallas_call x2, Pallas kernels, triangle(): pl.pallas_call(functools.partial(triangle_kernel, outgoing, groups, parts...  402 us
    pallas_call x1, Pallas kernels, body(): pl.pallas_call(middle_kernel, grid=grid, in_specs=[smem, smem, pixels, pl...  38.2 us
    pallas_call x1, Pallas kernels, body(): pl.pallas_call(last_kernel, grid=grid, in_specs=[pixels, planes] + [whole...  20.9 us
    pallas_call x1, Pallas kernels, body(): pl.pallas_call(first_kernel, grid=grid, in_specs=[smem, smem, pixels] + [...  19.1 us

profile of v5, /device:TPU:13, one launch (start us, length us, event | category | flops | bytes accessed | tf_op | source)
XLA Modules:
  0.0 490.6 jit_solution(12222619940622003882)
XLA Ops:
  0.7 0.6 dynamic_slice.15
  1.3 0.6 dynamic_slice.13.real_s
  1.9 0.8 dynamic_slice.14
  2.6 0.8 copy.18.col_chain
  3.4 1.3 dynamic_slice.12.chain_s
  4.7 1.1 copy.17
  5.8 0.7 slice_bitcast_fusion
  6.6 19.1 %first_projection.1 = (bf16[128,64,256]{2,1,0:T(8,128)(2,1)}, bf16[128,64,256]{2,1,0:T(8,128)(2,1)}) custom-call(s32[64]{0:T(128)} %dynamic_slice.12.chain_s, f32[64]{0:T(128)} %dynamic_slice.13.real_s, f32[64,256,128]{2,1,0:T(8,128)} %pair.3, s32[256,1]{1,0:T(8,128)} %copy.18.col_chain, f32[1,256]{1,0:T(1,128)} %bitcast.27, f32[1,128]{1,0:T(1,128)} %bitcast.30, ...), custom_call_target="tpu_custom_call" | custom-call | tf_op jit(solution)/shard_map/first_projection/pallas_call | solution.py:349
  25.6 0.0 copy-start
  25.6 0.0 copy-start.1
  25.6 0.0 copy-start.2
  25.7 0.0 copy-start.3
  25.7 198.4 %outgoing_product.1.mixed = bf16[128,64,256]{2,1,0:T(8,128)(2,1)} custom-call(bf16[128,64,256]{2,1,0:T(8,128)(2,1)} %get-tuple-element.10.left, bf16[128,64,256]{2,1,0:T(8,128)(2,1)} %get-tuple-element.11.right), custom_call_target="tpu_custom_call" | custom-call | tf_op jit(solution)/shard_map/outgoing_product/pallas_call | solution.py:302
  224.1 0.0 copy-done
  224.1 0.0 copy-done.1
  224.1 0.7 slice_bitcast_fusion.2
  224.8 0.0 copy-done.2
  224.8 0.7 copy.20.hid_gain
  225.5 0.0 copy-done.3
  225.5 0.7 copy.21.hid_bias
  226.2 38.2 %update_and_projection.1 = (f32[64,256,128]{2,1,0:T(8,128)}, bf16[128,64,256]{2,1,0:T(8,128)(2,1)}, bf16[128,64,256]{2,1,0:T(8,128)(2,1)}) custom-call(s32[64]{0:T(128)} %dynamic_slice.12.chain_s, f32[64]{0:T(128)} %dynamic_slice.13.real_s, f32[64,256,128]{2,1,0:T(8,128)} %pair.3, bf16[128,64,256]{2,1,0:T(8,128)(2,1)} %outgoing_product.1.mixed, ...), custom_call_target="tpu_custom_call" | custom-call | tf_op jit(solution)/shard_map/update_and_projection/pallas_call | solution.py:360
  264.5 203.8 %incoming_product.1.mixed = bf16[128,64,256]{2,1,0:T(8,128)(2,1)} custom-call(bf16[128,64,256]{2,1,0:T(8,128)(2,1)} %get-tuple-element.13.left, bf16[128,64,256]{2,1,0:T(8,128)(2,1)} %get-tuple-element.14.right), custom_call_target="tpu_custom_call" | custom-call | tf_op jit(solution)/shard_map/incoming_product/pallas_call | solution.py:302
  468.2 0.7 copy.22.hid_gain
  469.0 0.7 copy.23.hid_bias
  469.7 20.9 %last_update.1 = f32[64,256,128]{2,1,0:T(8,128)} custom-call(f32[64,256,128]{2,1,0:T(8,128)} %get-tuple-element.12.state_in, bf16[128,64,256]{2,1,0:T(8,128)(2,1)} %incoming_product.1.mixed, f32[2,128]{1,0:T(2,128)} %gain.5, f32[2,128]{1,0:T(2,128)} %bias.5, bf16[128,128]{1,0:T(8,128)(2,1)} %get-tuple-element.26.gate_w, f32[128,1]{1,0:T(8,128)} %copy.22.hid_gain, ...), custom_call_target="tpu_custom_call" | custom-call | tf_op jit(solution)/shard_map/last_update/pallas_call | solution.py:374
  (3 shorter events, 0.0 us)
Async XLA Ops:
  25.6 198.4 %copy-start = (bf16[2,128,128]{2,1,0:T(8,128)(2,1)S(1)}, bf16[2,128,128]{2,1,0:T(8,128)(2,1)}, u32[]{:S(2)}) copy-start(bf16[2,128,128]{2,1,0:T(8,128)(2,1)} %param.21) | copy-start | bytes 196612
  25.6 198.5 %copy-start.1 = (bf16[2,128,128]{2,1,0:T(8,128)(2,1)S(1)}, bf16[2,128,128]{2,1,0:T(8,128)(2,1)}, u32[]{:S(2)}) copy-start(bf16[2,128,128]{2,1,0:T(8,128)(2,1)} %param.18) | copy-start | bytes 196612
  25.6 199.1 %copy-start.2 = (f32[2,128]{1,0:T(2,128)S(1)}, f32[2,128]{1,0:T(2,128)}, u32[]{:S(2)}) copy-start(f32[2,128]{1,0:T(2,128)} %param.19) | copy-start | bytes 3076
  25.7 199.9 %copy-start.3 = (f32[2,128]{1,0:T(2,128)S(1)}, f32[2,128]{1,0:T(2,128)}, u32[]{:S(2)}) copy-start(f32[2,128]{1,0:T(2,128)} %param.20) | copy-start | bytes 3076
